TPU v7x, 32 devices: a whole 2x2x4 slice. The times are simulated.
32 devices in a mesh: dp: 8 (over z, y), cuts: 4 (over x, core).
Axes of the slice: x: 2, y: 2, z: 4, core: 2. Of those that a mesh axis runs over, the one named last changes fastest.
Arguments:
- tokens: bfloat16 [128, 6144], P('dp', 'cuts'), may hold values from -6 to 6
- out_grad: bfloat16 [128, 6144], P('dp', 'cuts'), may hold values from -6 to 6
- gate_values: float32 [128, 2], P('dp'), may hold values from 0.2 to 1
- routing: int32 [128, 2], P('dp'), may hold values from 0 to 7, all different within a row; in each aligned block of 16 rows (0 to 15, 16 to 31, ...) at most 8 rows name the same one
- gate_weight: bfloat16 [8, 6144, 11264], P('dp', None, 'cuts'), may hold values from -0.078125 to 0.078125
- up_weight: bfloat16 [8, 6144, 11264], P('dp', None, 'cuts'), may hold values from -0.078125 to 0.078125
- down_weight: bfloat16 [8, 11264, 6144], P('dp', 'cuts'), may hold values from -0.0546875 to 0.0546875
Outputs:
- mixed: bfloat16 [128, 6144], P('dp', 'cuts')
- token_grad: bfloat16 [128, 6144], P('dp', 'cuts')
Inputs may be any that keep to these rules, and one draw needn't show every extreme that they name: `routing`: each row names 2 different experts; in each aligned block of 16 rows (the rows of one index of dp) no expert is named by more than 8 rows, and in some block one expert is named by exactly 8 rows.
All inputs are finite; a program needn't handle non-finite values.
Results may differ from a plain program's by a relative error of at most 0.019.
Values may be sent and summed in bfloat16 or wider, within the bound.
A program may use at most 192 MiB of HBM per device.

v0:
```python
import jax
import jax.numpy as jnp
from jax import lax
from jax.sharding import PartitionSpec as P

E = 8
TOPK = 2
CAP = 8


def slot_table(routing):
    experts = routing.reshape(-1)
    onehot = (experts[:, None] == jnp.arange(E, dtype=jnp.int32)[None, :]).astype(jnp.int32)
    before = jnp.cumsum(onehot, axis=0) - onehot
    position = jnp.sum(before * onehot, axis=1)
    slots = experts * CAP + position
    select = (jnp.arange(E * CAP, dtype=jnp.int32)[:, None] == slots[None, :]).astype(jnp.bfloat16)
    return (slots, select)


def expert_pass(rows_x, rows_dy, wg, wu, w2):
    contract = (((1,), (1,)), ((), ()))
    gate_pre = jnp.dot(rows_x, wg, preferred_element_type=jnp.float32)
    up_pre = jnp.dot(rows_x, wu, preferred_element_type=jnp.float32)
    sigma = jax.nn.sigmoid(gate_pre)
    silu = gate_pre * sigma
    hidden = (silu * up_pre).astype(jnp.bfloat16)
    out_part = jnp.dot(hidden, w2, preferred_element_type=jnp.float32).astype(jnp.bfloat16)
    hid_grad = lax.dot_general(rows_dy, w2, contract, preferred_element_type=jnp.float32)
    gate_grad = (hid_grad * up_pre * sigma * (1.0 + gate_pre * (1.0 - sigma))).astype(jnp.bfloat16)
    up_grad = (hid_grad * silu).astype(jnp.bfloat16)
    in_part = lax.dot_general(gate_grad, wg, contract, preferred_element_type=jnp.float32)
    in_part = in_part + lax.dot_general(up_grad, wu, contract, preferred_element_type=jnp.float32)
    return (out_part, in_part.astype(jnp.bfloat16))


def build_buffers(feat_x, feat_dy, gate_values, select, owners):
    width = feat_x.shape[1]
    pairs_x = jnp.repeat(feat_x, TOPK, axis=0)
    pairs_dy = (gate_values[:, :, None] * feat_dy[:, None, :].astype(jnp.float32)).astype(
        jnp.bfloat16
    )
    pairs_dy = pairs_dy.reshape(-1, width)
    send_x = jnp.dot(select, pairs_x, preferred_element_type=jnp.float32).astype(jnp.bfloat16)
    send_dy = jnp.dot(select, pairs_dy, preferred_element_type=jnp.float32).astype(jnp.bfloat16)
    send_x = jnp.repeat(send_x.reshape(E, CAP, width), owners, axis=0)
    send_dy = jnp.repeat(send_dy.reshape(E, CAP, width), owners, axis=0)
    return (send_x, send_dy)


def combine(back_y, back_dx, slots, gate_values, owners):
    width = back_y.shape[2]
    tok_rows = gate_values.shape[0]
    sum_y = jnp.sum(back_y.astype(jnp.float32).reshape(E, owners, CAP, width), axis=1).reshape(
        E * CAP, width
    )
    sum_dx = jnp.sum(back_dx.astype(jnp.float32).reshape(E, owners, CAP, width), axis=1).reshape(
        E * CAP, width
    )
    rows_y = jnp.take(sum_y, slots, axis=0).reshape(tok_rows, TOPK, width)
    rows_dx = jnp.take(sum_dx, slots, axis=0).reshape(tok_rows, TOPK, width)
    mixed_part = jnp.sum(rows_y * gate_values[:, :, None], axis=1)
    grad_part = jnp.sum(rows_dx, axis=1)
    return (mixed_part, grad_part)


def on_device(tokens, out_grad, gate_values, routing, gate_weight, up_weight, down_weight):
    owners = lax.axis_size("dp") // E
    slots, select = slot_table(routing)
    wg = gate_weight[0]
    wu = up_weight[0]
    w2 = down_weight[0]
    whole_x, whole_dy = (
        lax.all_gather(tokens, "cuts", axis=1, tiled=True),
        lax.all_gather(out_grad, "cuts", axis=1, tiled=True),
    )
    send_x, send_dy = build_buffers(whole_x, whole_dy, gate_values, select, owners)
    piece_x = lax.all_to_all(send_x, "dp", split_axis=0, concat_axis=0, tiled=True)
    piece_dy = lax.all_to_all(send_dy, "dp", split_axis=0, concat_axis=0, tiled=True)
    sources, count, width = piece_x.shape
    out_part, in_part = expert_pass(
        piece_x.reshape(-1, width), piece_dy.reshape(-1, width), wg, wu, w2
    )
    out_part = out_part.reshape(sources, count, width)
    in_part = in_part.reshape(sources, count, width)
    back_y = lax.all_to_all(out_part, "dp", split_axis=0, concat_axis=0, tiled=True)
    back_dx = lax.all_to_all(in_part, "dp", split_axis=0, concat_axis=0, tiled=True)
    mixed_part, grad_part = combine(back_y, back_dx, slots, gate_values, owners)
    mixed, token_grad = (
        lax.psum_scatter(
            mixed_part.astype(jnp.bfloat16), "cuts", scatter_dimension=1, tiled=True
        ).astype(jnp.float32),
        lax.psum_scatter(
            grad_part.astype(jnp.bfloat16), "cuts", scatter_dimension=1, tiled=True
        ).astype(jnp.float32),
    )
    return (mixed.astype(jnp.bfloat16), token_grad.astype(jnp.bfloat16))


def solution(mesh):
    return jax.shard_map(
        on_device,
        mesh=mesh,
        in_specs=(
            P("dp", "cuts"),
            P("dp", "cuts"),
            P("dp", None),
            P("dp", None),
            P("dp", None, "cuts"),
            P("dp", None, "cuts"),
            P("dp", "cuts", None),
        ),
        out_specs=(P("dp", "cuts"), P("dp", "cuts")),
        check_vma=False,
    )
```

profile of v0, /device:TPU:0, one launch (start us, length us, event | category | flops | bytes accessed | tf_op | source)
XLA Modules:
  0.0 232.3 jit_solution(10809664713030813949)
XLA Ops:
  7.2 0.8 copy.12
  8.3 7.0 %all_gather.6 = bf16[16,6144]{1,0:T(8,128)(2,1)S(1)} all-gather(bf16[16,1536]{1,0:T(8,128)(2,1)} %param.9), channel_id=1, replica_groups=mesh['dp'=8,'cuts'=4] {'cuts'}, dimensions={1}, use_global_device_ids=true | all-gather | bytes 245760 | tf_op jit(solution)/shard_map/all_gather | solution.py:74
  15.4 0.2 broadcast_in_dim.8
  15.8 1.3 fusion.27
  17.0 6.0 %all-to-all-start = ((bf16[8,8,6144]{2,1,0:T(8,128)(2,1)}), bf16[8,8,6144]{2,1,0:T(8,128)(2,1)S(1)}, u32[]{:S(2)}, u32[]{:S(2)}) async-start(bf16[8,8,6144]{2,1,0:T(8,128)(2,1)} %fusion.27), calls=%async_computation | async-start | bytes 1572864 | tf_op jit(solution)/shard_map/all_to_all | solution.py:78
  23.1 0.8 copy.13
  23.9 5.8 %all_gather.7 = bf16[16,6144]{1,0:T(8,128)(2,1)S(1)} all-gather(bf16[16,1536]{1,0:T(8,128)(2,1)} %param.10), channel_id=1, replica_groups=mesh['dp'=8,'cuts'=4] {'cuts'}, dimensions={1}, use_global_device_ids=true | all-gather | bytes 245760 | tf_op jit(solution)/shard_map/all_gather | solution.py:75
  29.7 0.3 mul.69
  30.0 0.5 mul.70
  30.6 1.3 fusion.28
  31.9 11.8 %all-to-all-done = bf16[8,8,6144]{2,1,0:T(8,128)(2,1)S(1)} async-done(((bf16[8,8,6144]{2,1,0:T(8,128)(2,1)}), bf16[8,8,6144]{2,1,0:T(8,128)(2,1)S(1)}, u32[]{:S(2)}, u32[]{:S(2)}) %all-to-all-start) | async-done | bytes 786464 | tf_op jit(solution)/shard_map/all_to_all | solution.py:78
  43.7 3.7 %all-to-all-start.2 = ((bf16[8,8,6144]{2,1,0:T(8,128)(2,1)}), bf16[8,8,6144]{2,1,0:T(8,128)(2,1)S(1)}, u32[]{:S(2)}, u32[]{:S(2)}) async-start(bf16[8,8,6144]{2,1,0:T(8,128)(2,1)} %fusion.28), calls=%async_computation.3 | async-start | bytes 1572864 | tf_op jit(solution)/shard_map/all_to_all | solution.py:79
  47.5 14.0 %fusion.10 = f32[64,2816]{1,0:T(8,128)S(1)} fusion(bf16[1,6144,2816]{2,1,0:T(8,128)(2,1)} %param.13, bf16[8,8,6144]{2,1,0:T(8,128)(2,1)S(1)} %all-to-all-done), kind=kOutput, calls=%fused_computation.12 | convolution fusion | flops 2214592512 | bytes 36110336 | tf_op jit(solution)/shard_map/dot_general | solution.py:23
  61.4 6.3 %all-to-all-done.2 = bf16[8,8,6144]{2,1,0:T(8,128)(2,1)S(1)} async-done(((bf16[8,8,6144]{2,1,0:T(8,128)(2,1)}), bf16[8,8,6144]{2,1,0:T(8,128)(2,1)S(1)}, u32[]{:S(2)}, u32[]{:S(2)}) %all-to-all-start.2) | async-done | bytes 786464 | tf_op jit(solution)/shard_map/all_to_all | solution.py:79
  67.7 15.8 %fusion = f32[64,2816]{1,0:T(8,128)S(1)} fusion(bf16[1,2816,6144]{2,1,0:T(8,128)(2,1)} %param.15, bf16[8,8,6144]{2,1,0:T(8,128)(2,1)S(1)} %all-to-all-done.2), kind=kOutput, calls=%fused_computation.2 | convolution fusion | flops 2214592512 | bytes 36110336 | tf_op jit(solution)/shard_map/dot_general | solution.py:29
  83.5 15.7 %fusion.4 = f32[64,6144]{1,0:T(8,128)S(1)} fusion(bf16[1,6144,2816]{2,1,0:T(8,128)(2,1)} %param.14, f32[64,2816]{1,0:T(8,128)S(1)} %fusion, f32[64,2816]{1,0:T(8,128)S(1)} %fusion.10), kind=kOutput, calls=%fused_computation.6 | convolution fusion | flops 2215673856 | bytes 37617664 | tf_op jit(solution)/shard_map/dot_general | solution.py:33
  99.3 13.9 %fusion.6 = f32[64,2816]{1,0:T(8,128)S(1)} fusion(bf16[1,6144,2816]{2,1,0:T(8,128)(2,1)} %param.14, bf16[8,8,6144]{2,1,0:T(8,128)(2,1)S(1)} %all-to-all-done), kind=kOutput, calls=%fused_computation.8 | convolution fusion | flops 2214592512 | bytes 36110336 | tf_op jit(solution)/shard_map/dot_general | solution.py:24
  113.2 17.4 %fusion.24 = bf16[8,8,6144]{2,1,0:T(8,128)(2,1)} fusion(f32[64,6144]{1,0:T(8,128)S(1)} %fusion.4, bf16[1,6144,2816]{2,1,0:T(8,128)(2,1)} %param.13, f32[64,2816]{1,0:T(8,128)S(1)} %fusion.10, f32[64,2816]{1,0:T(8,128)S(1)} %fusion, f32[64,2816]{1,0:T(8,128)S(1)} %fusion.6), kind=kOutput, calls=%fused_computation.20 | convolution fusion | flops 2217181184 | bytes 39124992 | tf_op jit(solution)/shard_map/dot_general | solution.py:32
  130.6 3.8 %all-to-all-start.3 = ((bf16[8,8,6144]{2,1,0:T(8,128)(2,1)}), bf16[8,8,6144]{2,1,0:T(8,128)(2,1)S(1)}, u32[]{:S(2)}, u32[]{:S(2)}) async-start(bf16[8,8,6144]{2,1,0:T(8,128)(2,1)} %fusion.24), calls=%async_computation.4 | async-start | bytes 1572864 | tf_op jit(solution)/shard_map/all_to_all | solution.py:87
  134.4 15.0 %fusion.21 = bf16[8,8,6144]{2,1,0:T(8,128)(2,1)} fusion(bf16[1,2816,6144]{2,1,0:T(8,128)(2,1)} %param.15, f32[64,2816]{1,0:T(8,128)S(1)} %fusion.6, f32[64,2816]{1,0:T(8,128)S(1)} %fusion.10), kind=kOutput, calls=%fused_computation.19 | convolution fusion | flops 2216067072 | bytes 36831232 | tf_op jit(solution)/shard_map/dot_general | solution.py:28
  149.4 5.2 %all-to-all-done.3 = bf16[8,8,6144]{2,1,0:T(8,128)(2,1)S(1)} async-done(((bf16[8,8,6144]{2,1,0:T(8,128)(2,1)}), bf16[8,8,6144]{2,1,0:T(8,128)(2,1)S(1)}, u32[]{:S(2)}, u32[]{:S(2)}) %all-to-all-start.3) | async-done | bytes 786464 | tf_op jit(solution)/shard_map/all_to_all | solution.py:87
  154.6 3.6 %all-to-all-start.1 = ((bf16[8,8,6144]{2,1,0:T(8,128)(2,1)}), bf16[8,8,6144]{2,1,0:T(8,128)(2,1)S(1)}, u32[]{:S(2)}, u32[]{:S(2)}) async-start(bf16[8,8,6144]{2,1,0:T(8,128)(2,1)} %fusion.21), calls=%async_computation.1 | async-start | bytes 1572864 | tf_op jit(solution)/shard_map/all_to_all | solution.py:86
  158.3 0.8 gather_fusion.1
  159.1 19.4 %all-to-all-done.1 = bf16[8,8,6144]{2,1,0:T(8,128)(2,1)S(1)} async-done(((bf16[8,8,6144]{2,1,0:T(8,128)(2,1)}), bf16[8,8,6144]{2,1,0:T(8,128)(2,1)S(1)}, u32[]{:S(2)}, u32[]{:S(2)}) %all-to-all-start.1) | async-done | bytes 786464 | tf_op jit(solution)/shard_map/all_to_all | solution.py:86
  178.6 0.8 gather_fusion
  179.4 1.1 broadcast_select_fusion
  180.5 1.6 reshape.74
  182.1 1.7 multiply_reduce_fusion
  183.9 0.5 reshape.79
  184.4 1.7 reduce_sum.29
  186.1 16.6 %reduce-scatter.3.cloned.1.call-done = bf16[16,1536]{1,0:T(8,128)(2,1)} async-done(((bf16[16,6144]{1,0:T(8,128)(2,1)}), bf16[16,1536]{1,0:T(8,128)(2,1)}) %reduce-scatter.3.cloned.1.call-update) | async-done | bytes 49168 | tf_op jit(solution)/shard_map/reduce_scatter | solution.py:90
  202.7 22.8 %reduce-scatter.5.cloned.1.call-done = bf16[16,1536]{1,0:T(8,128)(2,1)} async-done(((bf16[16,6144]{1,0:T(8,128)(2,1)}), bf16[16,1536]{1,0:T(8,128)(2,1)}) %reduce-scatter.5.cloned.1.call-update) | async-done | bytes 49168 | tf_op jit(solution)/shard_map/reduce_scatter | solution.py:93
  (15 shorter events, 1.0 us)
Async XLA Ops:
  17.0 26.7 %all-to-all-start = ((bf16[8,8,6144]{2,1,0:T(8,128)(2,1)}), bf16[8,8,6144]{2,1,0:T(8,128)(2,1)S(1)}, u32[]{:S(2)}, u32[]{:S(2)}) async-start(bf16[8,8,6144]{2,1,0:T(8,128)(2,1)} %fusion.27), calls=%async_computation | async-start | bytes 1572864 | tf_op jit(solution)/shard_map/all_to_all | solution.py:78
  43.7 24.0 %all-to-all-start.2 = ((bf16[8,8,6144]{2,1,0:T(8,128)(2,1)}), bf16[8,8,6144]{2,1,0:T(8,128)(2,1)S(1)}, u32[]{:S(2)}, u32[]{:S(2)}) async-start(bf16[8,8,6144]{2,1,0:T(8,128)(2,1)} %fusion.28), calls=%async_computation.3 | async-start | bytes 1572864 | tf_op jit(solution)/shard_map/all_to_all | solution.py:79
  130.6 23.9 %all-to-all-start.3 = ((bf16[8,8,6144]{2,1,0:T(8,128)(2,1)}), bf16[8,8,6144]{2,1,0:T(8,128)(2,1)S(1)}, u32[]{:S(2)}, u32[]{:S(2)}) async-start(bf16[8,8,6144]{2,1,0:T(8,128)(2,1)} %fusion.24), calls=%async_computation.4 | async-start | bytes 1572864 | tf_op jit(solution)/shard_map/all_to_all | solution.py:87
  154.6 23.9 %all-to-all-start.1 = ((bf16[8,8,6144]{2,1,0:T(8,128)(2,1)}), bf16[8,8,6144]{2,1,0:T(8,128)(2,1)S(1)}, u32[]{:S(2)}, u32[]{:S(2)}) async-start(bf16[8,8,6144]{2,1,0:T(8,128)(2,1)} %fusion.21), calls=%async_computation.1 | async-start | bytes 1572864 | tf_op jit(solution)/shard_map/all_to_all | solution.py:86
  158.1 44.6 %reduce-scatter.3.cloned.1.call-start = ((), (), s32[]{:S(2)}) async-start(), calls=%async_computation.6 | async-start | bytes 245760 | tf_op jit(solution)/shard_map/reduce_scatter | solution.py:90
  183.8 41.6 %reduce-scatter.5.cloned.1.call-start = ((), (), s32[]{:S(2)}) async-start(), calls=%async_computation.7 | async-start | bytes 245760 | tf_op jit(solution)/shard_map/reduce_scatter | solution.py:93
Sparse Core Ops, SparseCore 0:
  184.0 18.6 reduce-scatter.2
  205.7 19.7 reduce-scatter.4
where the time goes:
time: 233 us; the launch traced here: 232 us
  matrix products  94.4 us (41%)
  waiting for transfers between devices  82.1 us (35%)
  starting transfers between devices  17.2 us (7%)
  between operations  14.2 us (6%)
  blocking collectives  12.9 us (6%)
  local copies, waits for them, and re-layouts  6.56 us (3%)
  other arithmetic  5.02 us (2%)
    reduce_scatter x1, waiting for transfers between devices, on_device(): lax.psum_scatter(grad_part.astype(jnp.bfloat16), 'cuts', scatter_dimensio...  22.8 us
    all_to_all x1, waiting for transfers between devices, on_device(): lax.all_to_all(out_part, 'dp', split_axis=0, concat_axis=0, tiled=True)  19.4 us
    dot_general x1, matrix products, expert_pass(): lax.dot_general(gate_grad, wg, contract, preferred_element_type=jnp.float32)  17.4 us
    reduce_scatter x1, waiting for transfers between devices, on_device(): lax.psum_scatter(mixed_part.astype(jnp.bfloat16), 'cuts', scatter_dimensi...  16.6 us
    dot_general x1, matrix products, expert_pass(): lax.dot_general(rows_dy, w2, contract, preferred_element_type=jnp.float32)  15.8 us
    dot_general x1, matrix products, expert_pass(): lax.dot_general(up_grad, wu, contract, preferred_element_type=jnp.float32)  15.7 us
    dot_general x1, matrix products, expert_pass(): jnp.dot(hidden, w2, preferred_element_type=jnp.float32).astype(jnp.bfloat16)  15 us
    dot_general x1, matrix products, expert_pass(): gate_pre = jnp.dot(rows_x, wg, preferred_element_type=jnp.float32)  14 us
  transfers between devices with their start and end apart: 6, of which 6 were waited for; matrix products, arithmetic and copies ran while one was open for 15% of the time, Pallas kernels for 0%

commit v1 on v0

v1 whole, which is shorter than its diff:
```python
import functools

import jax
import jax.numpy as jnp
from jax import lax
from jax.experimental import pallas as pl
from jax.experimental.pallas import tpu as pltpu
from jax.sharding import PartitionSpec as P

E = 8
TOPK = 2
CAP = 8
MESH = pl.DeviceIdType.MESH
F32 = jnp.float32
BF16 = jnp.bfloat16
NT = (((1,), (1,)), ((), ()))


def slot_table(routing):
    experts = routing.reshape(-1)
    pairs = experts.shape[0]
    at = jnp.arange(pairs, dtype=jnp.int32)
    same = (experts[:, None] == experts[None, :]) & (at[None, :] < at[:, None])
    slots = (experts * CAP + jnp.sum(same.astype(jnp.int32), axis=1)).reshape(routing.shape)
    numbers = jnp.arange(E * CAP, dtype=jnp.int32)
    takes = [(numbers[:, None] == slots[:, k][None, :]).astype(BF16) for k in range(TOPK)]
    gives = [(slots[:, k][:, None] == numbers[None, :]).astype(BF16) for k in range(TOPK)]
    return takes + gives


def body(
    n, cuts, tile, depth,
    x_ref, dy_ref, gate_ref, take0, take1, give0, give1, wg_hbm, wu_hbm, w2_hbm,
    mixed_ref, grad_ref,
    wg, wu, w2, send, rx, rows_x, rows_dy, acc_y, acc_dx,
    core_tx, core_rx, x_tx, x_rx, own, back_tx, back_rx,
    w_sem, a_send, a_recv, b_send, b_recv, c_send, c_recv, f_send, f_recv,
    r1_send, r1_recv, r2_send, r2_recv, r3_send, r3_recv,
):
    me, cut = lax.axis_index("dp"), lax.axis_index("cuts")
    nx = cuts // 2
    core, xx = lax.rem(cut, 2), lax.div(cut, 2)
    owners = n // E
    width = x_ref.shape[1]
    tiles = wg_hbm.shape[2] // tile
    mate = (me, xx * 2 + 1 - core)

    def fetch(t, slot):
        cols = pl.ds(t * tile, tile) if tiles == 1 else pl.ds(pl.multiple_of(t * tile, tile), tile)
        return (
            pltpu.make_async_copy(wg_hbm.at[0, :, cols], wg.at[slot], w_sem.at[0, slot]),
            pltpu.make_async_copy(wu_hbm.at[0, :, cols], wu.at[slot], w_sem.at[1, slot]),
            pltpu.make_async_copy(w2_hbm.at[0, cols, :], w2.at[slot], w_sem.at[2, slot]),
        )

    for t in range(min(depth, tiles)):
        for copy in fetch(t, t):
            copy.start()

    barrier = pltpu.get_barrier_semaphore()

    def greet(j, carry):
        pl.semaphore_signal(barrier, inc=1, device_id=(lax.rem(me + j, n), cut), device_id_type=MESH)
        return carry

    lax.fori_loop(1, n, greet, 0)
    pl.semaphore_signal(barrier, inc=1, device_id=mate, device_id_type=MESH)
    for i in range(1, nx):
        pl.semaphore_signal(
            barrier, inc=1, device_id=(me, lax.rem(xx + i, nx) * 2 + core), device_id_type=MESH
        )

    x = x_ref[...]
    dy = dy_ref[...].astype(F32)
    gate = gate_ref[...]
    sent_x = jnp.dot(take0[...] + take1[...], x, preferred_element_type=F32)
    sent_dy = jnp.dot(take0[...], (gate[:, 0:1] * dy).astype(BF16), preferred_element_type=F32)
    sent_dy += jnp.dot(take1[...], (gate[:, 1:2] * dy).astype(BF16), preferred_element_type=F32)
    send[...] = jnp.concatenate(
        [sent_x.reshape(E, CAP, width), sent_dy.reshape(E, CAP, width)], axis=1
    ).astype(BF16)
    rx[cut, me] = send[lax.div(me, owners)]

    pl.semaphore_wait(barrier, (n - 1) + 1 + (nx - 1))

    def remote(src, dst, send_sem, recv_sem, device):
        return pltpu.make_async_remote_copy(
            src_ref=src, dst_ref=dst, send_sem=send_sem, recv_sem=recv_sem,
            device_id=device, device_id_type=MESH,
        )

    def source(j):
        return lax.rem(me - j + n, n)

    def copy_a(j):
        to = lax.rem(me + j, n)
        return remote(send.at[lax.div(to, owners)], rx.at[cut, me], a_send.at[j], a_recv.at[j], (to, cut))

    def copy_b(j):
        s = source(j)
        return remote(rx.at[cut, s], rx.at[cut, s], b_send.at[j], b_recv.at[j], mate)

    def copy_c(i, j):
        s = source(j)
        to = (me, lax.rem(xx + i, nx) * 2 + core)
        return remote(rx.at[cut, s], rx.at[cut, s], c_send.at[i - 1, j], c_recv.at[i - 1, j], to)

    def copy_f(i, j):
        s = source(j)
        part = lax.rem(xx - i + nx, nx) * 2 + core
        return remote(rx.at[part, s], rx.at[part, s], f_send.at[i - 1, j], f_recv.at[i - 1, j], mate)

    def loop(start, stop, step):
        def run(j, carry):
            step(j)
            return carry

        lax.fori_loop(start, stop, run, 0)

    def spread(j):
        for i in range(1, nx):
            copy_c(i, j).start()
        copy_b(j).start()

    def arrive(j):
        copy_a(j).wait_recv()
        spread(j)

    def forward(j):
        for i in range(1, nx):
            copy_c(i, j).wait_recv()
            copy_f(i, j).start()

    def both(j):
        arrive(j)
        forward(j - 2)

    def landed(j):
        copy_b(j).wait_recv()
        for i in range(1, nx):
            copy_f(i, j).wait_recv()

    loop(1, n, lambda j: copy_a(j).start())
    spread(0)
    arrive(1)
    acc_y[...] = jnp.zeros_like(acc_y)
    acc_dx[...] = jnp.zeros_like(acc_dx)
    loop(2, n, both)
    loop(n - 2, n, forward)
    loop(0, n, landed)

    for part in range(cuts):
        cols = slice(part * width, (part + 1) * width)
        got = rx[part].astype(F32)
        rows_x[:, cols] = got[:, :CAP].reshape(n * CAP, width).astype(BF16)
        rows_dy[:, cols] = got[:, CAP:].reshape(n * CAP, width).astype(BF16)

    def hidden_tile(t):
        slot = lax.rem(t, depth)
        for copy in fetch(t, slot):
            copy.wait()
        gate_pre = jnp.dot(rows_x[...], wg[slot], preferred_element_type=F32)
        up_pre = jnp.dot(rows_x[...], wu[slot], preferred_element_type=F32)
        hid_grad = lax.dot_general(rows_dy[...], w2[slot], NT, preferred_element_type=F32)
        sigma = 1.0 / (1.0 + jnp.exp(-gate_pre))
        silu = gate_pre * sigma
        hidden = (silu * up_pre).astype(BF16)
        gate_grad = (hid_grad * up_pre * sigma * (1.0 + gate_pre * (1.0 - sigma))).astype(BF16)
        up_grad = (hid_grad * silu).astype(BF16)
        for part in range(cuts):
            cols = slice(part * width, (part + 1) * width)
            acc_y[:, cols] += jnp.dot(hidden, w2[slot, :, cols], preferred_element_type=F32)
            acc_dx[:, cols] += lax.dot_general(
                gate_grad, wg[slot, cols, :], NT, preferred_element_type=F32
            ) + lax.dot_general(up_grad, wu[slot, cols, :], NT, preferred_element_type=F32)

        @pl.when(t + depth < tiles)
        def _():
            for copy in fetch(t + depth, slot):
                copy.start()

    loop(0, tiles, hidden_tile)

    def partial(part):
        cols = pl.ds(pl.multiple_of(part * width, 128), width)
        return jnp.concatenate(
            [acc_y[:, cols].reshape(n, CAP, width), acc_dx[:, cols].reshape(n, CAP, width)], axis=1
        )

    def copy_r1(p):
        return remote(core_tx.at[p], core_rx.at[p], r1_send.at[p], r1_recv.at[p], mate)

    def copy_r2(i, d):
        to = (me, lax.rem(xx + i, nx) * 2 + core)
        return remote(
            x_tx.at[i - 1, d], x_rx.at[i - 1, d], r2_send.at[i - 1, d], r2_recv.at[i - 1, d], to
        )

    def copy_r3(j):
        to = lax.rem(me + j, n)
        return remote(back_tx.at[to], back_rx.at[me], r3_send.at[j], r3_recv.at[j], (to, cut))

    for i in list(range(1, nx)) + [0]:
        p = lax.rem(xx + i, nx)
        core_tx[p] = partial(p * 2 + 1 - core).astype(BF16)
        copy_r1(p).start()
    for i in list(range(1, nx)) + [0]:
        p = lax.rem(xx + i, nx)
        mine = partial(p * 2 + core)
        copy_r1(p).wait_recv()
        mine = mine + core_rx[p].astype(F32)
        if i == 0:
            own[...] = mine
        else:
            x_tx[i - 1] = mine.astype(BF16)
            loop(1, n + 1, lambda j, i=i: copy_r2(i, lax.rem(me + j, n)).start())

    def total(d):
        value = own[d]
        for i in range(1, nx):
            copy_r2(i, d).wait_recv()
            value = value + x_rx[i - 1, d].astype(F32)
        return value.astype(BF16)

    def give_back(j):
        d = lax.rem(me + j, n)
        back_tx[d] = total(d)
        copy_r3(j).start()

    loop(1, n, give_back)
    back_rx[me] = total(me)
    loop(1, n, lambda j: copy_r3(j).wait_recv())

    back = back_rx[...].astype(F32).reshape(E, owners, 2 * CAP, width)
    mixed = jnp.zeros(mixed_ref.shape, F32)
    grad = jnp.zeros(grad_ref.shape, F32)
    for o in range(owners):
        y = back[:, o, :CAP].reshape(E * CAP, width).astype(BF16)
        dx = back[:, o, CAP:].reshape(E * CAP, width).astype(BF16)
        mixed += gate[:, 0:1] * jnp.dot(give0[...], y, preferred_element_type=F32)
        mixed += gate[:, 1:2] * jnp.dot(give1[...], y, preferred_element_type=F32)
        grad += jnp.dot(give0[...] + give1[...], dx, preferred_element_type=F32)
    mixed_ref[...] = mixed.astype(BF16)
    grad_ref[...] = grad.astype(BF16)

    loop(1, n, lambda j: copy_a(j).wait_send())
    loop(0, n, lambda j: copy_b(j).wait_send())
    for i in range(1, nx):
        loop(0, n, lambda j, i=i: copy_c(i, j).wait_send())
        loop(0, n, lambda j, i=i: copy_f(i, j).wait_send())
        loop(0, n, lambda j, i=i: copy_r2(i, j).wait_send())
    for p in range(nx):
        copy_r1(p).wait_send()
    loop(1, n, lambda j: copy_r3(j).wait_send())


def on_device(n, cuts, tokens, out_grad, gate_values, routing, gate_weight, up_weight, down_weight):
    tables = slot_table(routing)
    count, width = tokens.shape
    _, model, hid = gate_weight.shape
    tile = 256 if hid % 256 == 0 else hid
    depth = min(4, hid // tile)
    nx, rows = cuts // 2, n * CAP
    chunk = (2 * CAP, width)
    dma = pltpu.SemaphoreType.DMA
    vmem = pl.BlockSpec(memory_space=pltpu.VMEM)
    hbm = pl.BlockSpec(memory_space=pl.ANY)
    out = jax.ShapeDtypeStruct((count, width), BF16)
    return pl.pallas_call(
        functools.partial(body, n, cuts, tile, depth),
        out_shape=(out, out),
        in_specs=[vmem] * 7 + [hbm] * 3,
        out_specs=(vmem, vmem),
        scratch_shapes=[
            pltpu.VMEM((depth, model, tile), BF16),
            pltpu.VMEM((depth, model, tile), BF16),
            pltpu.VMEM((depth, tile, model), BF16),
            pltpu.VMEM((E,) + chunk, BF16),
            pltpu.VMEM((cuts, n) + chunk, BF16),
            pltpu.VMEM((rows, model), BF16),
            pltpu.VMEM((rows, model), BF16),
            pltpu.VMEM((rows, model), F32),
            pltpu.VMEM((rows, model), F32),
            pltpu.VMEM((nx, n) + chunk, BF16),
            pltpu.VMEM((nx, n) + chunk, BF16),
            pltpu.VMEM((nx - 1, n) + chunk, BF16),
            pltpu.VMEM((nx - 1, n) + chunk, BF16),
            pltpu.VMEM((n,) + chunk, F32),
            pltpu.VMEM((n,) + chunk, BF16),
            pltpu.VMEM((n,) + chunk, BF16),
            dma((3, depth)),
            dma((n,)), dma((n,)),
            dma((n,)), dma((n,)),
            dma((nx - 1, n)), dma((nx - 1, n)),
            dma((nx - 1, n)), dma((nx - 1, n)),
            dma((nx,)), dma((nx,)),
            dma((nx - 1, n)), dma((nx - 1, n)),
            dma((n,)), dma((n,)),
        ],
        compiler_params=pltpu.CompilerParams(
            collective_id=0, has_side_effects=True, vmem_limit_bytes=62 * 1024 * 1024
        ),
        cost_estimate=pl.CostEstimate(
            flops=12 * rows * model * hid, bytes_accessed=6 * model * hid, transcendentals=rows * hid
        ),
    )(tokens, out_grad, gate_values, *tables, gate_weight, up_weight, down_weight)


def solution(mesh):
    return jax.shard_map(
        functools.partial(on_device, mesh.shape["dp"], mesh.shape["cuts"]),
        mesh=mesh,
        in_specs=(
            P("dp", "cuts"),
            P("dp", "cuts"),
            P("dp", None),
            P("dp", None),
            P("dp", None, "cuts"),
            P("dp", None, "cuts"),
            P("dp", "cuts", None),
        ),
        out_specs=(P("dp", "cuts"), P("dp", "cuts")),
        check_vma=False,
    )
```

time: 233 us -> 112 us (0.48)
  Pallas kernels: 0 us -> 104 us
  matrix products: 94.4 us -> 0 us
  waiting for transfers between devices: 82.1 us -> 0 us
  starting transfers between devices: 17.2 us -> 0 us
  between operations: 14.2 us -> 0.65 us
  blocking collectives: 12.9 us -> 0 us
  other arithmetic: 5.02 us -> 2.17 us
    pallas_call x0 -> x1, Pallas kernels: none -> 104 us  [on_device(): pl.pallas_call(functools.partial(body, n, cuts, tile, depth), out_shape=(...]
    dot_general x8 -> x0, matrix products: 94.4 us -> none  [the longest x1 17.4 us: expert_pass(): lax.dot_general(gate_grad, wg, contract, preferred_element_type=jnp.float32)]
    all_to_all x4 -> x0, waiting for transfers between devices: 42.7 us -> none  [the longest x1 19.4 us: on_device(): lax.all_to_all(out_part, 'dp', split_axis=0, concat_axis=0, tiled=True)]
    reduce_scatter x2 -> x0, waiting for transfers between devices: 39.4 us -> none  [the longest x1 22.8 us: on_device(): lax.psum_scatter(grad_part.astype(jnp.bfloat16), 'cuts', scatter_dimensio...]
    all_to_all x4 -> x0, starting transfers between devices: 17.1 us -> none  [the longest x1 6.05 us: on_device(): lax.all_to_all(send_x, 'dp', split_axis=0, concat_axis=0, tiled=True)]
    all_gather x2 -> x0, blocking collectives: 12.9 us -> none  [the longest x1 7.05 us: on_device(): lax.all_gather(tokens, 'cuts', axis=1, tiled=True)]
    unnamed x2 -> x4, local copies, waits for them, and re-layouts: 1.51 us -> 4.95 us
    reduce_sum x3 -> x1, other arithmetic: 3.61 us -> 0.18 us  [slot_table(): jnp.sum(same.astype(jnp.int32), axis=1)]
  transfers between devices with their start and end apart: 6 -> 0, of which waited for: 6 -> 0; matrix products, arithmetic and copies ran while one was open for 15% -> 0% of each run, Pallas kernels for 0% -> 0%
where the time goes in v1:
time: 112 us
  Pallas kernels  104 us (93%)
  local copies, waits for them, and re-layouts  5.21 us (5%)
  other arithmetic  2.17 us (2%)
    pallas_call x1, Pallas kernels, on_device(): pl.pallas_call(functools.partial(body, n, cuts, tile, depth), out_shape=(...  104 us
    unnamed x4, local copies, waits for them, and re-layouts  4.95 us

profile of v1, /device:TPU:0, one launch (start us, length us, event | category | flops | bytes accessed | tf_op | source)
XLA Modules:
  0.0 111.8 jit_solution(12477058191629870449)
XLA Ops:
  0.6 1.4 %copy.23.gate_ref = f32[16,2]{1,0:T(8,128)} copy(f32[16,2]{0,1:T(2,128)} %param.9) | data formatting | bytes 256 | tf_op args[2]
  2.0 0.8 copy.21
  2.7 0.1 eq.72
  2.8 0.2 convert_reduce_fusion
  3.0 0.1 reduce_sum.12
  3.1 0.1 copy.22
  3.2 0.7 multiply_add_fusion
  3.9 0.7 fusion.3
  4.6 0.6 fusion
  5.2 103.8 %shard_map.86 = (bf16[16,1536]{1,0:T(8,128)(2,1)}, bf16[16,1536]{1,0:T(8,128)(2,1)}) custom-call(bf16[16,1536]{1,0:T(8,128)(2,1)} %x_ref.1, bf16[16,1536]{1,0:T(8,128)(2,1)} %dy_ref.1, f32[16,2]{1,0:T(8,128)} %copy.23.gate_ref, bf16[64,16]{1,0:T(8,128)(2,1)} %get-tuple-element.4.take0, bf16[64,16]{1,0:T(8,128)(2,1)} %get-tuple-element.5.take1, ...), custom_call_target="tpu_custom_call" | custom-call | flops 13287555072 | bytes 103809024 | tf_op jit(solution)/shard_map/pallas_call | solution.py:269
  109.0 1.4 %copy.26 = bf16[16,1536]{1,0:T(8,128)(2,1)} copy(bf16[16,1536]{1,0:T(8,128)(2,1)} %get-tuple-element.10) | data formatting | bytes 98304
  110.4 1.4 %copy.27 = bf16[16,1536]{1,0:T(8,128)(2,1)} copy(bf16[16,1536]{1,0:T(8,128)(2,1)} %get-tuple-element.11) | data formatting | bytes 98304
  (1 shorter events, 0.0 us)

commit v2 on v1

--- a/solution.py
+++ b/solution.py
@@ -13,7 +13,6 @@
 MESH = pl.DeviceIdType.MESH
 F32 = jnp.float32
 BF16 = jnp.bfloat16
-NT = (((1,), (1,)), ((), ()))
 
 
 def slot_table(routing):
@@ -32,7 +31,7 @@
     n, cuts, tile, depth,
     x_ref, dy_ref, gate_ref, take0, take1, give0, give1, wg_hbm, wu_hbm, w2_hbm,
     mixed_ref, grad_ref,
-    wg, wu, w2, send, rx, rows_x, rows_dy, acc_y, acc_dx,
+    wg, wu, w2, send, rx, rows_x, turned_dy, acc_y, acc_dx,
     core_tx, core_rx, x_tx, x_rx, own, back_tx, back_rx,
     w_sem, a_send, a_recv, b_send, b_recv, c_send, c_recv, f_send, f_recv,
     r1_send, r1_recv, r2_send, r2_recv, r3_send, r3_recv,
@@ -149,11 +148,18 @@
     loop(n - 2, n, forward)
     loop(0, n, landed)
 
+    rows = n * CAP
+    lanes = turned_dy.shape[1]
+
+    def turn(value, filler):
+        value = value if lanes == rows else jnp.concatenate([value, filler], axis=0)
+        return value.T.astype(BF16)
+
     for part in range(cuts):
         cols = slice(part * width, (part + 1) * width)
         got = rx[part].astype(F32)
         rows_x[:, cols] = got[:, :CAP].reshape(n * CAP, width).astype(BF16)
-        rows_dy[:, cols] = got[:, CAP:].reshape(n * CAP, width).astype(BF16)
+        turned_dy[cols, :] = turn(got[:, CAP:].reshape(rows, width), got[:, :CAP].reshape(rows, width))
 
     def hidden_tile(t):
         slot = lax.rem(t, depth)
@@ -161,18 +167,20 @@
             copy.wait()
         gate_pre = jnp.dot(rows_x[...], wg[slot], preferred_element_type=F32)
         up_pre = jnp.dot(rows_x[...], wu[slot], preferred_element_type=F32)
-        hid_grad = lax.dot_general(rows_dy[...], w2[slot], NT, preferred_element_type=F32)
+        hid_grad = jnp.dot(w2[slot], turned_dy[...], preferred_element_type=F32).T[:rows]
         sigma = 1.0 / (1.0 + jnp.exp(-gate_pre))
         silu = gate_pre * sigma
         hidden = (silu * up_pre).astype(BF16)
-        gate_grad = (hid_grad * up_pre * sigma * (1.0 + gate_pre * (1.0 - sigma))).astype(BF16)
-        up_grad = (hid_grad * silu).astype(BF16)
+        gate_grad = (hid_grad * up_pre * sigma * (1.0 + gate_pre * (1.0 - sigma)))
+        up_grad = hid_grad * silu
+        turned_gate = turn(gate_grad, up_grad)
+        turned_up = turn(up_grad, gate_grad)
         for part in range(cuts):
             cols = slice(part * width, (part + 1) * width)
             acc_y[:, cols] += jnp.dot(hidden, w2[slot, :, cols], preferred_element_type=F32)
-            acc_dx[:, cols] += lax.dot_general(
-                gate_grad, wg[slot, cols, :], NT, preferred_element_type=F32
-            ) + lax.dot_general(up_grad, wu[slot, cols, :], NT, preferred_element_type=F32)
+            acc_dx[cols, :] += jnp.dot(
+                wg[slot, cols, :], turned_gate, preferred_element_type=F32
+            ) + jnp.dot(wu[slot, cols, :], turned_up, preferred_element_type=F32)
 
         @pl.when(t + depth < tiles)
         def _():
@@ -184,7 +192,8 @@
     def partial(part):
         cols = pl.ds(pl.multiple_of(part * width, 128), width)
         return jnp.concatenate(
-            [acc_y[:, cols].reshape(n, CAP, width), acc_dx[:, cols].reshape(n, CAP, width)], axis=1
+            [acc_y[:, cols].reshape(n, CAP, width), acc_dx[cols, :].T[:rows].reshape(n, CAP, width)],
+            axis=1,
         )
 
     def copy_r1(p):
@@ -261,6 +270,7 @@
     tile = 256 if hid % 256 == 0 else hid
     depth = min(4, hid // tile)
     nx, rows = cuts // 2, n * CAP
+    lanes = rows if rows % 128 == 0 else 2 * rows
     chunk = (2 * CAP, width)
     dma = pltpu.SemaphoreType.DMA
     vmem = pl.BlockSpec(memory_space=pltpu.VMEM)
@@ -278,9 +288,9 @@
             pltpu.VMEM((E,) + chunk, BF16),
             pltpu.VMEM((cuts, n) + chunk, BF16),
             pltpu.VMEM((rows, model), BF16),
-            pltpu.VMEM((rows, model), BF16),
+            pltpu.VMEM((model, lanes), BF16),
             pltpu.VMEM((rows, model), F32),
-            pltpu.VMEM((rows, model), F32),
+            pltpu.VMEM((model, lanes), F32),
             pltpu.VMEM((nx, n) + chunk, BF16),
             pltpu.VMEM((nx, n) + chunk, BF16),
             pltpu.VMEM((nx - 1, n) + chunk, BF16),

time: 112 us -> 96.9 us (0.87)
  Pallas kernels: 104 us -> 88.6 us
    pallas_call x1, Pallas kernels: 104 us -> 88.6 us  [on_device(): pl.pallas_call(functools.partial(body, n, cuts, tile, depth), out_shape=(...]
where the time goes in v2:
time: 96.9 us; the launch traced here: 96.6 us
  Pallas kernels  88.6 us (91%)
  local copies, waits for them, and re-layouts  5.21 us (5%)
  other arithmetic  2.17 us (2%)
    pallas_call x1, Pallas kernels, on_device(): pl.pallas_call(functools.partial(body, n, cuts, tile, depth), out_shape=(...  88.6 us
    unnamed x4, local copies, waits for them, and re-layouts  4.95 us

profile of v2, /device:TPU:0, one launch (start us, length us, event | category | flops | bytes accessed | tf_op | source)
XLA Modules:
  0.0 96.6 jit_solution(2416655957666262273)
XLA Ops:
  0.6 1.4 %copy.23.gate_ref = f32[16,2]{1,0:T(8,128)} copy(f32[16,2]{0,1:T(2,128)} %param.9) | data formatting | bytes 256 | tf_op args[2]
  2.0 0.8 copy.21
  2.7 0.1 eq.72
  2.8 0.2 convert_reduce_fusion
  3.0 0.1 reduce_sum.12
  3.1 0.1 copy.22
  3.2 0.7 multiply_add_fusion
  3.9 0.7 fusion.3
  4.6 0.6 fusion
  5.2 88.6 %shard_map.86 = (bf16[16,1536]{1,0:T(8,128)(2,1)}, bf16[16,1536]{1,0:T(8,128)(2,1)}) custom-call(bf16[16,1536]{1,0:T(8,128)(2,1)} %x_ref.1, bf16[16,1536]{1,0:T(8,128)(2,1)} %dy_ref.1, f32[16,2]{1,0:T(8,128)} %copy.23.gate_ref, bf16[64,16]{1,0:T(8,128)(2,1)} %get-tuple-element.4.take0, bf16[64,16]{1,0:T(8,128)(2,1)} %get-tuple-element.5.take1, ...), custom_call_target="tpu_custom_call" | custom-call | flops 13287555072 | bytes 103809024 | tf_op jit(solution)/shard_map/pallas_call | solution.py:279
  93.8 1.4 %copy.26 = bf16[16,1536]{1,0:T(8,128)(2,1)} copy(bf16[16,1536]{1,0:T(8,128)(2,1)} %get-tuple-element.10) | data formatting | bytes 98304
  95.2 1.4 %copy.27 = bf16[16,1536]{1,0:T(8,128)(2,1)} copy(bf16[16,1536]{1,0:T(8,128)(2,1)} %get-tuple-element.11) | data formatting | bytes 98304
  (1 shorter events, 0.0 us)
